TPU v7x, 32 devices: a whole 2x2x4 slice. The times are simulated.
32 devices in a mesh: section: 2 (over x), dp: 4 (over z), tensor: 4 (over y, core).
Axes of the slice: x: 2, y: 2, z: 4, core: 2. Of those that a mesh axis runs over, the one named last changes fastest.
Arguments:
- embedded: bfloat16 [8192, 768], P('dp'), may hold values from -6 to 6
- segment: int32 [16, 512], P('dp'), may hold values from 0 to 5, never falling along the last dimension, each value on 1 to 256 neighbouring positions
- query_key_value_weight: bfloat16 [2, 3, 768, 768], P('section', None, None, 'tensor'), may hold values from -0.21875 to 0.21875
- attention_output_weight: bfloat16 [2, 768, 768], P('section', 'tensor'), may hold values from -1.75 to 1.75
- feedforward_up_weight: bfloat16 [2, 768, 3072], P('section', None, 'tensor'), may hold values from -0.21875 to 0.21875
- feedforward_down_weight: bfloat16 [2, 3072, 768], P('section', 'tensor'), may hold values from -0.109375 to 0.109375
- adapter_down_weight: bfloat16 [2, 2, 768, 8], P('section'), may hold values from -0.21875 to 0.21875
- adapter_up_weight: bfloat16 [2, 2, 8, 768], P('section', None, None, 'tensor'), may hold values from -0.625 to 0.625
- layer_norm_gain: float32 [2, 2, 768], P('section'), may hold values from 0.5 to 1.5
- layer_norm_bias: float32 [2, 2, 768], P('section'), may hold values from -1.75 to 1.75
- cotangent: bfloat16 [8192, 768], P('dp'), may hold values from -6 to 6
Outputs:
- layer_outs: bfloat16 [2, 8192, 768], P('section', 'dp')
- in_grads: bfloat16 [2, 8192, 768], P('section', 'dp')
- grad_a: float32 [2, 2, 768, 8], P('section')
- grad_b: float32 [2, 2, 8, 768], P('section', None, None, 'tensor')
Inputs may be any that keep to these rules, and one draw needn't show every extreme that they name: `segment`: within each pack the ids never fall, every id of the range occurs, each covers at most 256 rows and one covers exactly that many.
All inputs are finite; a program needn't handle non-finite values.
Results may differ from a plain program's by a relative error of at most 0.025.
Values may be sent and summed in bfloat16 or wider, within the bound.
A program may use at most 192 MiB of HBM per device.

v0:
```python
from functools import partial

import jax
import jax.numpy as jnp
from jax import lax
from jax.experimental import pallas as pl
from jax.experimental.pallas import tpu as pltpu
from jax.sharding import PartitionSpec as P

HEAD_DIM = 64
EPS = 1e-05
VMEM_LIMIT = 115 * 2**19
F32 = jnp.float32
BF16 = jnp.bfloat16
ANY = pl.BlockSpec(memory_space=pl.ANY)
VMEM = pl.BlockSpec(memory_space=pltpu.VMEM)
MESH = pl.DeviceIdType.MESH
SMEM = pl.BlockSpec(memory_space=pltpu.SMEM)


def nn(a, b):
    return jnp.dot(a, b, preferred_element_type=F32)


def nt(a, b):
    return lax.dot_general(a, b, (((1,), (1,)), ((), ())), preferred_element_type=F32)


def lane_mask(shape, low, high):
    lanes = lax.broadcasted_iota(jnp.int32, shape, len(shape) - 1)
    return (lanes >= low) & (lanes < high)


def normalize(total):
    average = jnp.mean(total, -1, keepdims=True)
    centred = total - average
    spread = jnp.mean(centred * centred, -1, keepdims=True)
    scaled = lax.rsqrt(spread + EPS)
    return centred * scaled, scaled


def normalize_back(normed, scaled, gains, incoming):
    weighted = incoming * gains
    return scaled * (
        weighted
        - jnp.mean(weighted, -1, keepdims=True)
        - normed * jnp.mean(weighted * normed, -1, keepdims=True)
    )


def neighbours():
    section, plane, tensor = (lax.axis_index(n) for n in ("section", "dp", "tensor"))
    turned = lax.rem(tensor + 2, 4)
    other = tensor + 1 - 2 * lax.rem(tensor, 2)
    paired = plane + 1 - 2 * lax.rem(plane, 2)
    return (
        (section, plane, other),
        (section, plane, turned),
        (section, paired, tensor),
        (1 - section, plane, tensor),
    )


def meet(devices):
    barrier = pltpu.get_barrier_semaphore()
    for device in devices:
        pl.semaphore_signal(barrier, inc=1, device_id=device, device_id_type=MESH)
    pl.semaphore_wait(barrier, len(devices))


def remote(src, dst, send, recv, device):
    return pltpu.make_async_remote_copy(
        src_ref=src,
        dst_ref=dst,
        send_sem=send,
        recv_sem=recv,
        device_id=device,
        device_id_type=MESH,
    )


def identity(n):
    rows = lax.broadcasted_iota(jnp.int32, (n, n), 0)
    return (rows == lax.broadcasted_iota(jnp.int32, (n, n), 1)).astype(BF16)


def blocks_of(rows, size):
    return [pl.ds(r, size) for r in range(0, rows, size)]


class Gather:
    cuts, ahead = 4, 3
    count = 1 + 2 * cuts + 3
    first_qkv = 1 + 2 * cuts

    def __init__(self, own, gathered, partners, sems):
        self.qkv, self.outw, self.up, self.down, self.adapt = own
        self.qkv_v, self.out_v, self.ff_v, self.adapt_v = gathered
        self.core, self.far, self.plane = partners
        self.send, self.recv, self.local = sems
        self.parity = lax.rem(lax.axis_index("dp"), 2)
        self.n_qkv, self.n_out = self.qkv.shape[1], self.outw.shape[0]
        self.n_ff, self.n_adapt = self.up.shape[0], self.adapt.shape[0]

    def part(self, c, slot, p):
        if c == 0:
            half = self.n_out // 2
            return self.out_v.at[pl.ds(slot * self.n_out + p * half, half)]
        if c >= self.first_qkv:
            half = self.n_qkv // 2
            return self.qkv_v.at[c - self.first_qkv, pl.ds(slot * self.n_qkv + p * half, half)]
        which, i = divmod(c - 1, self.cuts)
        half = self.n_ff // 2
        size = half // self.cuts
        return self.ff_v.at[which, slot, pl.ds(p * half + i * size, size)]

    def whole(self, i, slot):
        if i == 0:
            return self.qkv_v.at[:, pl.ds(slot * self.n_qkv, self.n_qkv)]
        if i == 1:
            return self.out_v.at[pl.ds(slot * self.n_out, self.n_out)]
        if i == 4:
            return self.adapt_v.at[pl.ds(slot * self.n_adapt, self.n_adapt)]
        return self.ff_v.at[i - 2, slot]

    def link(self, kind, c, src, dst, device):
        return remote(src, dst, self.send.at[kind, c], self.recv.at[kind, c], device)

    def over_far(self, c):
        return self.link(0, c, self.part(c, 0, self.parity), self.part(c, 2, self.parity), self.far)

    def to_plane(self, c):
        here = self.part(c, 2, self.parity)
        return self.link(1, c, here, here, self.plane)

    def from_plane(self, c):
        there = self.part(c, 2, 1 - self.parity)
        return self.link(1, c, there, there, self.plane)

    def near_to_core(self, c):
        p = self.parity
        return self.link(2, c, self.part(c, 2, p), self.part(c, 3, p), self.core)

    def other_to_core(self, c):
        p = 1 - self.parity
        return self.link(3, c, self.part(c, 2, p), self.part(c, 3, p), self.core)

    def load(self, i):
        own = (self.qkv, self.outw, self.up, self.down, self.adapt)[i]
        return pltpu.make_async_copy(own, self.whole(i, 0), self.local.at[i])

    def to_core(self, i):
        return self.link(4, i, self.whole(i, 0), self.whole(i, 1), self.core)

    def adapt_far(self):
        return self.link(5, 0, self.whole(4, 0), self.whole(4, 2), self.far)

    def adapt_core(self):
        return self.link(5, 1, self.whole(4, 2), self.whole(4, 3), self.core)

    def pump(self, begin, end):
        for c in range(begin, end):
            self.over_far(c).wait_recv()
            self.to_plane(c).start()
            self.near_to_core(c).start()
            if c + self.ahead < self.count:
                self.over_far(c + self.ahead).start()
            if c > 0:
                self.relay(c - 1)

    def relay(self, c):
        self.from_plane(c).wait_recv()
        self.other_to_core(c).start()

    def landed(self, begin, end):
        for c in range(begin, end):
            self.near_to_core(c).wait_recv()
            self.other_to_core(c).wait_recv()

    def sent(self):
        for c in range(self.count):
            for copy in (self.over_far(c), self.to_plane(c)):
                copy.wait_send()
            for copy in (self.near_to_core(c), self.other_to_core(c)):
                copy.wait_send()
        for i in range(5):
            self.to_core(i).wait_send()
        self.adapt_far().wait_send()
        self.adapt_core().wait_send()


def middle(h, adapt_down):
    rank = adapt_down.shape[0] // 2
    mid = nt(h, adapt_down[...]).astype(BF16)
    is_query = lane_mask(mid.shape, 0, rank)
    double = mid * jnp.asarray(2.0, BF16)
    zero = jnp.zeros((), BF16)
    return mid, jnp.where(is_query, double, zero), jnp.where(is_query, zero, double)


def project(h_v, adapt_down, w, ready):
    for part in blocks_of(h_v.shape[0], 256):
        ready(part)
        h = h_v[part]
        mid, mid_q, mid_v = middle(h, adapt_down)
        w.mid_t[:, part] = nt(identity(mid.shape[1]), mid).astype(BF16)
        for s, (ref, low) in enumerate(((w.q_v, mid_q), (w.k_v, None), (w.v_v, mid_v))):
            value = nt(h, w.qkv_v[s])
            if low is not None:
                value = value + nt(low, w.adapt_v[...])
            value = value.astype(BF16)
            span = ref.shape[2]
            for g in range(ref.shape[0]):
                ref[g, part] = value[:, g * span : (g + 1) * span]


def attend(q_v, k, v, bias, give):
    rows, span = k.shape
    chunk = 256
    zero = jnp.zeros((), BF16)
    for part in blocks_of(rows, chunk):
        q_c = q_v[part] * jnp.asarray(HEAD_DIM**-0.5, BF16)
        ctx = jnp.zeros((chunk, span), F32)
        inverse = jnp.zeros((chunk, span), F32)
        weights = []
        for e in range(span // HEAD_DIM):
            low = e * HEAD_DIM
            of_head = lane_mask(q_c.shape, low, low + HEAD_DIM)
            v_e = jnp.where(lane_mask(v.shape, low, low + HEAD_DIM), v, zero)
            s = nt(jnp.where(of_head, q_c, zero), k) + bias[part]
            weight = jnp.exp(s - jnp.max(s, -1, keepdims=True))
            scale = 1.0 / jnp.sum(weight, -1, keepdims=True)
            weight = weight.astype(BF16)
            ctx = ctx + nn(weight, v_e) * scale
            inverse = jnp.where(of_head, scale, inverse)
            give(part, e, weight, None)
        give(part, None, ctx.astype(BF16), inverse)


def attention_out(h_v, context, gains, biases, w, keep):
    groups, rows, span = context.shape
    for part in blocks_of(rows, 256):
        total = h_v[part].astype(F32)
        for g in range(groups):
            total = total + nn(context[g, part], w.out_v[g * span : (g + 1) * span])
        normed, scaled = normalize(total)
        if keep:
            w.n1_v[part] = normed
            w.s1_v[part] = scaled
        first = normed * gains[0:1] + biases[0:1]
        w.acc[part] = first
        w.low_v[part] = first.astype(BF16)


def feedforward_up(w, keep, ready):
    def step(slot, carry):
        ready(slot)
        for part in blocks_of(w.low_v.shape[0], 128):
            pre = nn(w.low_v[part], w.ff_v[0, slot])
            cdf = 0.5 + 0.5 * lax.erf(pre * (0.5**0.5))
            w.act_v[slot, part] = (pre * cdf).astype(BF16)
            if keep:
                density = jnp.exp(pre * pre * -0.5) * 0.3989422804014327
                w.slope_v[slot, part] = (cdf + pre * density).astype(BF16)
        return carry

    lax.fori_loop(0, w.act_v.shape[0], step, 0)


def backward(w, gains, adapt_down, incoming, give, sums):
    rows = w.acc.shape[0]
    slots = w.ff_v.shape[1]
    groups, _, span = w.q_v.shape
    for part in blocks_of(rows, 256):
        back = normalize_back(w.n2_v[part], w.s2_v[part], gains[1:2], incoming(part))
        w.acc[part] = back
        w.low_v[part] = back.astype(BF16)

        def step(slot, carry):
            dact = nt(w.low_v[part], w.ff_v[1, slot])
            w.act_v[slot, part] = (dact * w.slope_v[slot, part].astype(F32)).astype(BF16)
            return carry

        lax.fori_loop(0, slots, step, 0)
        total = w.acc[part]
        for slot in range(slots):
            total = total + nt(w.act_v[slot, part], w.ff_v[0, slot])
        back = normalize_back(w.n1_v[part], w.s1_v[part], gains[0:1], total)
        w.acc[part] = back
        dctx = nt(back.astype(BF16), w.out_v[...])
        for g in range(groups):
            scaled = dctx[:, g * span : (g + 1) * span] * w.inv_v[g, part]
            w.dctx_v[g, part] = scaled.astype(BF16)
    heads = span // HEAD_DIM
    factor = HEAD_DIM**-0.5

    def group(g, carry):
        q, k, v = w.q_v[g], w.k_v[g], w.v_v[g]
        dctx, ctx = w.dctx_v[g], w.ctx_v[g].astype(F32)
        q_t, dctx_t = q.T, dctx.T
        zero = jnp.zeros((), BF16)
        dq = jnp.zeros((rows, span), F32)
        dk_t, dv_t = [], []
        for e in range(heads):
            low, high = e * HEAD_DIM, (e + 1) * HEAD_DIM
            of_head = lane_mask((rows, span), low, high)
            weight = w.p_v[g * heads + e]
            dctx_e = jnp.where(of_head, dctx, zero)
            delta = jnp.sum(dctx_e.astype(F32) * ctx, -1, keepdims=True)
            ds = (weight.astype(F32) * (nt(dctx_e, v) - delta)).astype(BF16)
            dq = dq + nn(ds, jnp.where(of_head, k, zero))
            dk_t.append(nn(q_t[low:high], ds))
            dv_t.append(nn(dctx_t[low:high], weight))
        w.dq_v[g] = (dq * factor).astype(BF16)
        w.dk_v[g] = (jnp.concatenate(dk_t, 0) * factor).astype(BF16).T
        w.dv_v[g] = jnp.concatenate(dv_t, 0).astype(BF16).T
        return carry

    lax.fori_loop(0, groups, group, 0)
    rank = adapt_down.shape[0] // 2
    for part in blocks_of(rows, 256):
        dmid_q = dmid_v = 0.0
        for g in range(groups):
            cols = slice(g * span, (g + 1) * span)
            dmid_q = dmid_q + nn(w.dq_v[g, part], w.adapt_v[cols])
            dmid_v = dmid_v + nn(w.dv_v[g, part], w.adapt_v[cols])
        dmid = 2.0 * jnp.where(lane_mask(dmid_q.shape, 0, rank), dmid_q, dmid_v)
        w.dmid_v[part] = dmid.astype(BF16)
    sums()
    for part in blocks_of(rows, 128):
        total = w.acc[part]
        for g in range(groups):
            cols = slice(g * span, (g + 1) * span)
            for s, ref in enumerate((w.dq_v, w.dk_v, w.dv_v)):
                total = total + nn(ref[g, part], w.qkv_v[s, cols])
        give(part, (total + nn(w.dmid_v[part], adapt_down[...])).astype(BF16))


class Refs:
    def __init__(self, names, refs):
        self.__dict__.update(zip(names, refs, strict=True))


def whole_kernel(planes, names, *refs):
    embedded, segment, gains, biases, adapt_down, adapt, qkv, outw, up, down, cotangent = refs[:11]
    layer_outs, in_grads, down_out, up_out = refs[11:15]
    w = Refs(names, refs[15:])
    section, plane, tensor = (lax.axis_index(n) for n in ("section", "dp", "tensor"))
    core, far, paired, beyond = neighbours()
    turned = lax.rem(tensor + 2, 4)
    other = tensor + 1 - 2 * lax.rem(tensor, 2)
    across = lax.rem(other + 2, 4)
    indices = (other, turned, across)
    sides = tuple((section, plane, i) for i in indices)
    ring = [(section, lax.rem(plane + m, planes), tensor) for m in range(1, planes)]
    rows, width = w.h_v.shape
    groups = w.q_v.shape[0]

    own = pl.ds(tensor * rows, rows)
    gather = Gather(
        (qkv, outw, up, down, w.adapt_own),
        (w.qkv_v, w.out_v, w.ff_v, w.adapt_v),
        (core, far, paired),
        (w.send, w.recv, w.local),
    )
    for i in (1, 0, 2, 3):
        gather.load(i).start()
    pack_copies = [
        pltpu.make_async_copy(embedded.at[pl.ds(i * rows, rows)], w.slope_v.at[i], w.packs.at[i])
        for i in range(len(indices) + 1)
    ]
    for copy in pack_copies:
        copy.start()
    h_copy = pltpu.make_async_copy(embedded.at[own], w.h_v, w.local.at[5])
    h_copy.start()
    cot_copy = pltpu.make_async_copy(cotangent.at[own], w.cot_v, w.local.at[6])
    cot_copy.start()
    adapt_t = nt(identity(adapt.shape[1]), adapt[...]).astype(BF16)
    w.adapt_own[...] = adapt_t
    w.adapt_v[: adapt.shape[1]] = adapt_t
    meet((*sides, *ring, beyond))

    for i in (1, 2, 3, 0):
        gather.load(i).wait()
    for c in range(gather.ahead):
        gather.over_far(c).start()
    gather.adapt_far().start()
    for i in (4, 1, 2, 3, 0):
        gather.to_core(i).start()
    for copy in pack_copies:
        copy.wait()
    square = (rows, rows)
    diagonal = lax.broadcasted_iota(jnp.int32, square, 0) == lax.broadcasted_iota(
        jnp.int32, square, 1
    )
    piece = adapt.shape[1]

    def index_of(k):
        high = lax.rem(tensor // 2 + k // 2, 2)
        return 2 * high + lax.rem(lax.rem(tensor, 2) + lax.rem(k, 2), 2)

    def context_to(k):
        device = (section, plane, index_of(k))
        return remote(w.ctx_out.at[k], w.ctx_in.at[k], w.ctx_send.at[k], w.ctx_recv.at[k], device)

    def attend_pack(step, carry):
        k = 3 - step
        pack = index_of(k)
        ids = segment[pl.ds(pack, 1), :].astype(F32)
        column = jnp.sum(jnp.where(diagonal, ids, 0.0), -1, keepdims=True)
        w.bias[...] = jnp.where(column == ids, 0.0, -1e9)
        h = w.slope_v[pack]
        _, mid_q, mid_v = middle(h, adapt_down)
        w.q_own[...] = (nt(h, w.qkv_v[0, :piece]) + nt(mid_q, w.adapt_own[...])).astype(BF16)
        k_own = nt(h, w.qkv_v[1, :piece]).astype(BF16)
        v_own = (nt(h, w.qkv_v[2, :piece]) + nt(mid_v, w.adapt_own[...])).astype(BF16)

        def give(part, head, value, inverse):
            if head is None:
                w.ctx_out[k, part] = value

        attend(w.q_own, k_own, v_own, w.bias, give)

        @pl.when(step < 3)
        def _():
            context_to(k).start()

        for i in (1, 2, 3):

            @pl.when(step == i)
            def _():
                gather.pump(i - 1, i)

        return carry

    lax.fori_loop(0, 4, attend_pack, 0)
    w.ctx_in[0] = w.ctx_out[0]
    h_copy.wait()
    for k in (1, 2, 3):
        context_to(k).wait_recv()
    gather.to_core(1).wait_recv()
    gather.landed(0, 1)
    attention_out(w.h_v, w.ctx_in, gains, biases, w, False)
    gather.adapt_far().wait_recv()
    gather.adapt_core().start()
    ups, downs = 1 + gather.cuts, 1 + 2 * gather.cuts
    gather.pump(3, ups - 1)
    for i in (2, 3):
        gather.to_core(i).wait_recv()

    def rest_of_up(slot):
        @pl.when(slot == 2)
        def _():
            gather.pump(ups - 1, ups + 1)
            gather.landed(1, ups)

    feedforward_up(w, False, rest_of_up)
    gather.pump(ups + 1, ups + 2)
    for part in blocks_of(rows, 256):
        w.acc[part] += nn(w.act_v[0, part], w.ff_v[1, 0]) + nn(w.act_v[1, part], w.ff_v[1, 1])
    gather.pump(ups + 2, downs + 1)
    gather.landed(ups, downs)

    def hop(way, i, src, dst):
        return remote(src, dst, w.hop_send.at[way, i], w.hop_recv.at[way, i], beyond)

    pieces = blocks_of(rows, 128)
    for i, part in enumerate(pieces):
        total = w.acc[part] + nn(w.act_v[2, part], w.ff_v[1, 2]) + nn(w.act_v[3, part], w.ff_v[1, 3])
        w.hop_v[part] = (normalize(total)[0] * gains[1:2] + biases[1:2]).astype(BF16)
        hop(0, i, w.hop_v.at[part], w.recv_v.at[part]).start()
    gather.pump(downs + 1, gather.count)
    gather.relay(gather.count - 1)
    for i in (0, 4):
        gather.to_core(i).wait_recv()
    gather.adapt_core().wait_recv()
    gather.landed(downs, gather.count)

    def ready(part):
        for i in range(part.start // 128, (part.start + part.size) // 128):
            hop(0, i, w.hop_v.at[pieces[i]], w.recv_v.at[pieces[i]]).wait_recv()

        @pl.when(section == 1)
        def _():
            w.h_v[part] = w.recv_v[part]

    project(w.h_v, adapt_down, w, ready)

    def attend_group(g, carry):
        def give(part, head, value, inverse):
            if head is None:
                w.ctx_v[g, part] = value
                w.inv_v[g, part] = inverse
            else:
                w.p_v[g * (w.q_v.shape[2] // HEAD_DIM) + head, part] = value

        attend(w.q_v.at[g], w.k_v[g], w.v_v[g], w.bias, give)
        return carry

    lax.fori_loop(0, groups, attend_group, 0)
    attention_out(w.h_v, w.ctx_v, gains, biases, w, True)
    feedforward_up(w, True, lambda slot: None)

    def block(out, index, i):
        return out.at[pl.ds(index * rows + i * 128, 128)]

    def rows_far(n, src, out, i):
        return remote(
            src.at[pieces[i]], block(out, tensor, i), w.row_send.at[n, 0, i], w.row_recv.at[n, 0, i], far
        )

    def rows_core(n, src, out, i):
        return remote(
            src.at[pieces[i]], block(out, tensor, i), w.row_send.at[n, 1, i], w.row_recv.at[n, 1, i], core
        )

    def rows_mine(n, src, out, i):
        return pltpu.make_async_copy(src.at[pieces[i]], block(out, tensor, i), w.local.at[7 + 4 * n + i])

    def rows_relay(n, out, i):
        landed = block(out, turned, i)
        return remote(landed, landed, w.row_send.at[n, 2, i], w.row_recv.at[n, 2, i], core)

    def spread(n, src, out, i):
        for make in (rows_far, rows_core, rows_mine):
            make(n, src, out, i).start()

    def relay_rows(n, src, out, i):
        rows_far(n, src, out, i).wait_recv()
        rows_relay(n, out, i).start()

    def gathered(n, src, out):
        for i in range(len(pieces)):
            rows_core(n, src, out, i).wait_recv()
            rows_relay(n, out, i).wait_recv()
            for make in (rows_far, rows_core):
                make(n, src, out, i).wait_send()
            rows_relay(n, out, i).wait_send()
            rows_mine(n, src, out, i).wait()

    for i, part in enumerate(pieces):
        total = w.acc[part]
        for slot in range(w.ff_v.shape[1]):
            total = total + nn(w.act_v[slot, part], w.ff_v[1, slot])
        normed, scaled = normalize(total)
        w.n2_v[part] = normed
        w.s2_v[part] = scaled
        w.layer_v[part] = (normed * gains[1:2] + biases[1:2]).astype(BF16)
        spread(0, w.layer_v, layer_outs, i)

    cot_copy.wait()
    rank = adapt_down.shape[0] // 2

    def incoming(again, part):
        @pl.when(again == 1)
        def _():
            for i in range(part.start // 128, (part.start + part.size) // 128):
                hop(1, i, w.dh_v.at[pieces[i]], w.back_v.at[pieces[i]]).wait_recv()

        @pl.when(jnp.logical_and(again == 1, section == 0))
        def _():
            w.cot_v[part] = w.back_v[part]

        return w.cot_v[part].astype(F32)

    def summed(n, src, dst, device):
        return remote(src, dst, w.sum_send.at[n], w.sum_recv.at[n], device)

    def over_tensor(landing):
        copies = []
        for i, device in enumerate(sides):
            slot = indices[i] if landing else tensor
            for src, dst in (
                (w.grad_down, w.from_down.at[slot]),
                (w.grad_up.at[i + 1], w.from_up.at[i]),
            ):
                copies.append(summed(len(copies), src, dst, device))
        return copies

    def adapter_gradients(again):
        @pl.when(again == 1)
        def _():
            dmid_t = nt(identity(2 * rank), w.dmid_v[...]).astype(BF16)
            grad_down = nn(dmid_t, w.h_v[...])
            for j in range(2):
                w.grad_down[j] = grad_down[j * rank : (j + 1) * rank]
            up_q, up_v = (
                jnp.concatenate([2.0 * nn(w.mid_t[...], ref[g]) for g in range(groups)], 1)
                for ref in (w.dq_v, w.dv_v)
            )
            for i in range(len(sides) + 1):
                cols = slice(i * piece, (i + 1) * piece)
                w.grad_up[i, 0] = up_q[:rank, cols]
                w.grad_up[i, 1] = up_v[rank:, cols]
            w.from_down[tensor] = w.grad_down[...]
            for copy in over_tensor(False):
                copy.start()

    def hand_over(again, part, value):
        i = part.start // 128

        @pl.when(again == 0)
        def _():
            w.dh_v[part] = value
            hop(1, i, w.dh_v.at[part], w.back_v.at[part]).start()

        @pl.when(again == 1)
        def _():
            w.din_v[part] = value
            spread(1, w.din_v, in_grads, i)

    def back(again, carry):
        backward(
            w,
            gains,
            adapt_down,
            partial(incoming, again),
            partial(hand_over, again),
            partial(adapter_gradients, again),
        )

        @pl.when(again == 0)
        def _():
            for i in range(len(pieces)):
                relay_rows(0, w.layer_v, layer_outs, i)

        return carry

    lax.fori_loop(0, 2, back, 0)

    tensor_copies = over_tensor(True)
    for copy in tensor_copies:
        copy.wait()
    w.plane_down[plane] = w.from_down[0] + w.from_down[1] + w.from_down[2] + w.from_down[3]
    w.plane_up[plane] = w.grad_up[0] + w.from_up[0] + w.from_up[1] + w.from_up[2]
    base = len(tensor_copies)
    totals = (w.plane_down, w.plane_up)
    for m, device in enumerate(ring):
        for k, ref in enumerate(totals):
            summed(base + 2 * m + k, ref.at[plane], ref.at[plane], device).start()
    relay_rows(1, w.din_v, in_grads, 0)
    for m, device in enumerate(ring):
        source = lax.rem(plane + planes - m - 1, planes)
        for k, ref in enumerate(totals):
            summed(base + 2 * m + k, ref.at[source], ref.at[source], device).wait_recv()
    for m, device in enumerate(ring):
        for k, ref in enumerate(totals):
            summed(base + 2 * m + k, ref.at[plane], ref.at[plane], device).wait_send()
    down_total, up_total = w.plane_down[0], w.plane_up[0]
    for m in range(1, planes):
        down_total = down_total + w.plane_down[m]
        up_total = up_total + w.plane_up[m]
    up_out[...] = up_total
    down_out[...] = down_total
    for i in range(1, len(pieces)):
        relay_rows(1, w.din_v, in_grads, i)
    for way, src, dst in ((0, w.hop_v, w.recv_v), (1, w.dh_v, w.back_v)):
        for i, part in enumerate(pieces):
            hop(way, i, src.at[part], dst.at[part]).wait_send()
    gather.sent()
    for k in (1, 2, 3):
        context_to(k).wait_send()
    gathered(0, w.layer_v, layer_outs)
    gathered(1, w.din_v, in_grads)


def local(
    embedded,
    segment,
    query_key_value_weight,
    attention_output_weight,
    feedforward_up_weight,
    feedforward_down_weight,
    adapter_down_weight,
    adapter_up_weight,
    layer_norm_gain,
    layer_norm_bias,
    cotangent,
):
    slots, packs, planes = lax.axis_size("tensor"), segment.shape[0], lax.axis_size("dp")
    assert slots == 4 and packs == slots and planes % 2 == 0
    rows, width = segment.shape[1], embedded.shape[1]
    piece = query_key_value_weight.shape[3]
    wide = feedforward_up_weight.shape[2]
    assert wide == width
    rank = adapter_down_weight.shape[3]
    span = 256
    groups = width // span
    heads = width // HEAD_DIM

    def arr(shape, dtype):
        return jax.ShapeDtypeStruct(shape, dtype)

    low_rows = pltpu.VMEM((rows, width), BF16)
    full_rows = pltpu.VMEM((rows, width), F32)
    of_heads = pltpu.VMEM((groups, rows, span), BF16)
    of_hidden = pltpu.VMEM((slots, rows, wide), BF16)
    down_part = (2, rank, width)
    up_part = (2, rank, piece)
    sums = 2 * (slots - 1) + 2 * (planes - 1)
    scratch = dict(
        qkv_v=pltpu.VMEM((3, width, width), BF16),
        out_v=pltpu.VMEM((width, width), BF16),
        ff_v=pltpu.VMEM((2, slots, width, wide), BF16),
        adapt_v=pltpu.VMEM((width, 2 * rank), BF16),
        adapt_own=pltpu.VMEM((piece, 2 * rank), BF16),
        q_own=pltpu.VMEM((rows, piece), BF16),
        ctx_out=pltpu.VMEM((slots, rows, piece), BF16),
        ctx_in=pltpu.VMEM((slots, rows, piece), BF16),
        inv_v=pltpu.VMEM((groups, rows, span), F32),
        p_v=pltpu.VMEM((heads, rows, rows), BF16),
        s1_v=pltpu.VMEM((rows, 1), F32),
        s2_v=pltpu.VMEM((rows, 1), F32),
        bias=pltpu.VMEM((rows, rows), F32),
        mid_t=pltpu.VMEM((2 * rank, rows), BF16),
        dmid_v=pltpu.VMEM((rows, 2 * rank), BF16),
        grad_down=pltpu.VMEM(down_part, F32),
        grad_up=pltpu.VMEM((slots, *up_part), F32),
        from_down=pltpu.VMEM((slots, *down_part), F32),
        from_up=pltpu.VMEM((slots - 1, *up_part), F32),
        plane_down=pltpu.VMEM((planes, *down_part), F32),
        plane_up=pltpu.VMEM((planes, *up_part), F32),
        local=pltpu.SemaphoreType.DMA((15,)),
        packs=pltpu.SemaphoreType.DMA((packs,)),
        send=pltpu.SemaphoreType.DMA((6, Gather.count)),
        recv=pltpu.SemaphoreType.DMA((6, Gather.count)),
        ctx_send=pltpu.SemaphoreType.DMA((slots,)),
        ctx_recv=pltpu.SemaphoreType.DMA((slots,)),
        hop_send=pltpu.SemaphoreType.DMA((2, rows // 128)),
        hop_recv=pltpu.SemaphoreType.DMA((2, rows // 128)),
        row_send=pltpu.SemaphoreType.DMA((2, 3, rows // 128)),
        row_recv=pltpu.SemaphoreType.DMA((2, 3, rows // 128)),
        sum_send=pltpu.SemaphoreType.DMA((sums,)),
        sum_recv=pltpu.SemaphoreType.DMA((sums,)),
    )
    scratch |= dict.fromkeys(("h_v", "recv_v", "back_v", "cot_v", "low_v"), low_rows)
    scratch |= dict.fromkeys(("hop_v", "layer_v", "dh_v", "din_v"), low_rows)
    scratch |= dict.fromkeys(("acc", "n1_v", "n2_v"), full_rows)
    scratch |= dict.fromkeys(("q_v", "k_v", "v_v", "ctx_v"), of_heads)
    scratch |= dict.fromkeys(("dq_v", "dk_v", "dv_v", "dctx_v"), of_heads)
    scratch |= dict.fromkeys(("act_v", "slope_v"), of_hidden)
    layer_outs, in_grads, grad_a, grad_b = pl.pallas_call(
        partial(whole_kernel, planes, tuple(scratch)),
        name="encoder_layers",
        out_shape=[
            pltpu.VMEM((packs * rows, width), BF16),
            pltpu.VMEM((packs * rows, width), BF16),
            arr(down_part, F32),
            arr(up_part, F32),
        ],
        in_specs=[ANY] + [VMEM] * 5 + [ANY] * 5,
        out_specs=[VMEM] * 4,
        scratch_shapes=list(scratch.values()),
        compiler_params=pltpu.CompilerParams(
            vmem_limit_bytes=VMEM_LIMIT, collective_id=0, has_side_effects=True
        ),
        cost_estimate=pl.CostEstimate(
            flops=7 * 10**10, bytes_accessed=3 * 10**7, transcendentals=0
        ),
    )(
        embedded,
        segment,
        layer_norm_gain[0],
        layer_norm_bias[0],
        jnp.swapaxes(adapter_down_weight[0], 1, 2).reshape(2 * rank, width),
        adapter_up_weight[0].reshape(2 * rank, piece),
        jnp.swapaxes(query_key_value_weight[0], 1, 2),
        attention_output_weight[0],
        feedforward_up_weight[0],
        feedforward_down_weight[0],
        cotangent,
    )
    grad_a = jnp.swapaxes(grad_a, 1, 2)
    return (layer_outs[None], in_grads[None], grad_a[None], grad_b[None])


def solution(mesh):
    in_specs = (
        P("dp", None),
        P("dp", None),
        P("section", None, None, "tensor"),
        P("section", "tensor", None),
        P("section", None, "tensor"),
        P("section", "tensor", None),
        P("section", None, None, None),
        P("section", None, None, "tensor"),
        P("section", None, None),
        P("section", None, None),
        P("dp", None),
    )
    out_specs = (
        P("section", "dp", None),
        P("section", "dp", None),
        P("section", None, None, None),
        P("section", None, None, "tensor"),
    )
    return jax.shard_map(local, mesh=mesh, in_specs=in_specs, out_specs=out_specs, check_vma=False)
```

profile of v0, /device:TPU:0, one launch (start us, length us, event | category | flops | bytes accessed | tf_op | source)
XLA Modules:
  0.0 174.1 jit_solution(13562077790530903642)
XLA Ops:
  0.6 168.8 %encoder_layers.1 = (bf16[2048,768]{1,0:T(8,128)(2,1)S(1)}, bf16[2048,768]{1,0:T(8,128)(2,1)S(1)}, f32[2,8,768]{2,1,0:T(8,128)}, f32[2,8,192]{2,1,0:T(8,128)}) custom-call(bf16[2048,768]{1,0:T(8,128)(2,1)} %refs_0_.1, s32[4,512]{1,0:T(4,128)} %refs_1_.1, f32[2,768]{1,0:T(2,128)} %bitcast.30, f32[2,768]{1,0:T(2,128)} %bitcast.31, bf16[16,768]{1,0:T(8,128)(2,1)} %bitcast.28, ...), custom_call_target="tpu_custom_call" | custom-call | flops 70000001024 | bytes 30000000 | tf_op jit(solution)/shard_map/encoder_layers/pallas_call | solution.py:742
  169.5 1.7 copy.19
  171.2 0.0 copy-start
  171.2 0.0 copy-start.1
  171.2 1.7 copy.20
  172.8 0.0 copy-done
  172.8 0.6 copy.21
  173.4 0.0 copy-done.1
  173.4 0.6 copy.22
Async XLA Ops:
  171.2 1.7 copy-start
  171.2 2.3 %copy-start.1 = (f32[2,8,192]{2,1,0:T(8,128)S(1)}, f32[2,8,192]{2,1,0:T(8,128)}, u32[]{:S(2)}) copy-start(f32[2,8,192]{2,1,0:T(8,128)} %get-tuple-element.11) | copy-start | bytes 36868
where the time goes:
time: 175 us; the launch traced here: 174 us
  Pallas kernels  169 us (97%)
  local copies, waits for them, and re-layouts  4.56 us (3%)
    pallas_call x1, Pallas kernels, local(): pl.pallas_call(partial(whole_kernel, planes, tuple(scratch)), name='encod...  169 us
    unnamed x8, local copies, waits for them, and re-layouts  4.56 us

commit v1 on v0

--- a/solution.py
+++ b/solution.py
@@ -58,6 +58,7 @@
         (section, plane, turned),
         (section, paired, tensor),
         (1 - section, plane, tensor),
+        (1 - section, plane, turned),
     )
 
 
@@ -89,30 +90,34 @@
 
 
 class Gather:
-    cuts, ahead = 4, 3
-    count = 1 + 2 * cuts + 3
-    first_qkv = 1 + 2 * cuts
-
-    def __init__(self, own, gathered, partners, sems):
+    items, ahead, ahead_own = 8, 2, 8
+    through = 5
+
+    def __init__(self, own, gathered, resting, partners, sems):
         self.qkv, self.outw, self.up, self.down, self.adapt = own
         self.qkv_v, self.out_v, self.ff_v, self.adapt_v = gathered
-        self.core, self.far, self.plane = partners
+        self.resting_v = resting
+        self.core, self.far, self.plane, self.beyond, self.corner = partners
         self.send, self.recv, self.local = sems
         self.parity = lax.rem(lax.axis_index("dp"), 2)
         self.n_qkv, self.n_out = self.qkv.shape[1], self.outw.shape[0]
         self.n_ff, self.n_adapt = self.up.shape[0], self.adapt.shape[0]
 
-    def part(self, c, slot, p):
-        if c == 0:
-            half = self.n_out // 2
-            return self.out_v.at[pl.ds(slot * self.n_out + p * half, half)]
-        if c >= self.first_qkv:
-            half = self.n_qkv // 2
-            return self.qkv_v.at[c - self.first_qkv, pl.ds(slot * self.n_qkv + p * half, half)]
-        which, i = divmod(c - 1, self.cuts)
-        half = self.n_ff // 2
-        size = half // self.cuts
-        return self.ff_v.at[which, slot, pl.ds(p * half + i * size, size)]
+    def block(self, i, slot, third):
+        if i == 0:
+            size = self.n_out // 3
+            return self.out_v.at[pl.ds(slot * self.n_out + third * size, size)]
+        if i >= 5:
+            size = self.n_qkv // 3
+            return self.qkv_v.at[i - 5, pl.ds(slot * self.n_qkv + third * size, size)]
+        which, j = divmod(i - 1, 2)
+        rows = self.n_ff // 3
+        size = rows // 2
+        return self.ff_v.at[which, slot, pl.ds(third * rows + j * size, size)]
+
+    def resting(self, i):
+        size = self.n_out // 3 if i == 0 else self.n_ff // 6
+        return self.resting_v.at[i // 4, pl.ds(i % 4 * (self.n_ff // 6), size)]
 
     def whole(self, i, slot):
         if i == 0:
@@ -123,66 +128,111 @@
             return self.adapt_v.at[pl.ds(slot * self.n_adapt, self.n_adapt)]
         return self.ff_v.at[i - 2, slot]
 
-    def link(self, kind, c, src, dst, device):
-        return remote(src, dst, self.send.at[kind, c], self.recv.at[kind, c], device)
-
-    def over_far(self, c):
-        return self.link(0, c, self.part(c, 0, self.parity), self.part(c, 2, self.parity), self.far)
-
-    def to_plane(self, c):
-        here = self.part(c, 2, self.parity)
-        return self.link(1, c, here, here, self.plane)
-
-    def from_plane(self, c):
-        there = self.part(c, 2, 1 - self.parity)
-        return self.link(1, c, there, there, self.plane)
-
-    def near_to_core(self, c):
+    def link(self, kind, i, src, dst, device):
+        return remote(src, dst, self.send.at[kind, i], self.recv.at[kind, i], device)
+
+    def over_far(self, i):
         p = self.parity
-        return self.link(2, c, self.part(c, 2, p), self.part(c, 3, p), self.core)
-
-    def other_to_core(self, c):
-        p = 1 - self.parity
-        return self.link(3, c, self.part(c, 2, p), self.part(c, 3, p), self.core)
+        return self.link(0, i, self.block(i, 0, p), self.block(i, 2, p), self.far)
+
+    def to_plane(self, i, third):
+        here = self.block(i, 2, third)
+        return self.link(1, i, here, here, self.plane)
+
+    def pass_on(self, i, kind):
+        third = (self.parity, 1 - self.parity, 2)[kind]
+        return self.link(2 + kind, i, self.block(i, 2, third), self.block(i, 3, third), self.core)
+
+    def to_corner(self, i):
+        return self.link(7, i, self.block(i, 0, 2), self.resting(i), self.corner)
+
+    def to_beyond(self, i):
+        return self.link(8, i, self.resting(i), self.block(i, 2, 2), self.beyond)
+
+    def last_far(self, i):
+        return self.link(9, i, self.block(i, 0, 2), self.block(i, 2, 2), self.far)
+
+    def last_plane(self, i):
+        here = self.block(i, 2, 2)
+        return self.link(10, i, here, here, self.plane)
 
     def load(self, i):
         own = (self.qkv, self.outw, self.up, self.down, self.adapt)[i]
         return pltpu.make_async_copy(own, self.whole(i, 0), self.local.at[i])
 
     def to_core(self, i):
-        return self.link(4, i, self.whole(i, 0), self.whole(i, 1), self.core)
+        return self.link(5, i, self.whole(i, 0), self.whole(i, 1), self.core)
 
     def adapt_far(self):
-        return self.link(5, 0, self.whole(4, 0), self.whole(4, 2), self.far)
+        return self.link(6, 0, self.whole(4, 0), self.whole(4, 2), self.far)
 
     def adapt_core(self):
-        return self.link(5, 1, self.whole(4, 2), self.whole(4, 3), self.core)
-
-    def pump(self, begin, end):
-        for c in range(begin, end):
-            self.over_far(c).wait_recv()
-            self.to_plane(c).start()
-            self.near_to_core(c).start()
-            if c + self.ahead < self.count:
-                self.over_far(c + self.ahead).start()
-            if c > 0:
-                self.relay(c - 1)
-
-    def relay(self, c):
-        self.from_plane(c).wait_recv()
-        self.other_to_core(c).start()
-
-    def landed(self, begin, end):
-        for c in range(begin, end):
-            self.near_to_core(c).wait_recv()
-            self.other_to_core(c).wait_recv()
-
-    def sent(self):
-        for c in range(self.count):
-            for copy in (self.over_far(c), self.to_plane(c)):
-                copy.wait_send()
-            for copy in (self.near_to_core(c), self.other_to_core(c)):
-                copy.wait_send()
+        return self.link(6, 1, self.whole(4, 2), self.whole(4, 3), self.core)
+
+    def when_last(self, i, mine):
+        here = i % 2
+        return pl.when(self.parity == (here if mine else 1 - here))
+
+    def issue(self, i, through):
+        self.over_far(i).start()
+        if through:
+            self.to_corner(i).start()
+        else:
+
+            @self.when_last(i, True)
+            def _():
+                self.last_far(i).start()
+
+    def pump(self, i, through):
+        self.over_far(i).wait_recv()
+        self.to_plane(i, self.parity).start()
+        self.pass_on(i, 0).start()
+        if not through:
+
+            @self.when_last(i, True)
+            def _():
+                self.last_far(i).wait_recv()
+                self.last_plane(i).start()
+                self.pass_on(i, 2).start()
+
+    def relay(self, i, through):
+        self.to_plane(i, 1 - self.parity).wait_recv()
+        self.pass_on(i, 1).start()
+        if not through:
+
+            @self.when_last(i, False)
+            def _():
+                self.last_plane(i).wait_recv()
+                self.pass_on(i, 2).start()
+
+    def relay_last(self, i):
+        self.to_beyond(i).wait_recv()
+        self.pass_on(i, 2).start()
+
+    def help(self, i):
+        self.to_corner(i).wait_recv()
+        self.to_beyond(i).start()
+
+    def landed(self, *items):
+        for i in items:
+            for kind in range(3):
+                self.pass_on(i, kind).wait_recv()
+
+    def sent(self, section):
+        for i in range(self.items):
+            self.over_far(i).wait_send()
+            self.to_plane(i, self.parity).wait_send()
+            for kind in range(3):
+                self.pass_on(i, kind).wait_send()
+            if section == 0 and i < self.through:
+                self.to_corner(i).wait_send()
+            else:
+
+                @self.when_last(i, True)
+                def _():
+                    self.last_far(i).wait_send()
+                    self.last_plane(i).wait_send()
+
         for i in range(5):
             self.to_core(i).wait_send()
         self.adapt_far().wait_send()
@@ -346,7 +396,7 @@
     layer_outs, in_grads, down_out, up_out = refs[11:15]
     w = Refs(names, refs[15:])
     section, plane, tensor = (lax.axis_index(n) for n in ("section", "dp", "tensor"))
-    core, far, paired, beyond = neighbours()
+    core, far, paired, beyond, corner = neighbours()
     turned = lax.rem(tensor + 2, 4)
     other = tensor + 1 - 2 * lax.rem(tensor, 2)
     across = lax.rem(other + 2, 4)
@@ -360,7 +410,8 @@
     gather = Gather(
         (qkv, outw, up, down, w.adapt_own),
         (w.qkv_v, w.out_v, w.ff_v, w.adapt_v),
-        (core, far, paired),
+        w.act_v,
+        (core, far, paired, beyond, corner),
         (w.send, w.recv, w.local),
     )
     for i in (1, 0, 2, 3):
@@ -378,22 +429,27 @@
     adapt_t = nt(identity(adapt.shape[1]), adapt[...]).astype(BF16)
     w.adapt_own[...] = adapt_t
     w.adapt_v[: adapt.shape[1]] = adapt_t
-    meet((*sides, *ring, beyond))
+    meet((*sides, *ring, beyond, corner))
 
     for i in (1, 2, 3, 0):
         gather.load(i).wait()
-    for c in range(gather.ahead):
-        gather.over_far(c).start()
     gather.adapt_far().start()
     for i in (4, 1, 2, 3, 0):
         gather.to_core(i).start()
     for copy in pack_copies:
         copy.wait()
+    h_copy.wait()
     square = (rows, rows)
-    diagonal = lax.broadcasted_iota(jnp.int32, square, 0) == lax.broadcasted_iota(
-        jnp.int32, square, 1
-    )
     piece = adapt.shape[1]
+    pieces = blocks_of(rows, 128)
+
+    def mask(pack):
+        diagonal = lax.broadcasted_iota(jnp.int32, square, 0) == lax.broadcasted_iota(
+            jnp.int32, square, 1
+        )
+        ids = segment[pl.ds(pack, 1), :].astype(F32)
+        column = jnp.sum(jnp.where(diagonal, ids, 0.0), -1, keepdims=True)
+        w.bias[...] = jnp.where(column == ids, 0.0, -1e9)
 
     def index_of(k):
         high = lax.rem(tensor // 2 + k // 2, 2)
@@ -406,9 +462,7 @@
     def attend_pack(step, carry):
         k = 3 - step
         pack = index_of(k)
-        ids = segment[pl.ds(pack, 1), :].astype(F32)
-        column = jnp.sum(jnp.where(diagonal, ids, 0.0), -1, keepdims=True)
-        w.bias[...] = jnp.where(column == ids, 0.0, -1e9)
+        mask(pack)
         h = w.slope_v[pack]
         _, mid_q, mid_v = middle(h, adapt_down)
         w.q_own[...] = (nt(h, w.qkv_v[0, :piece]) + nt(mid_q, w.adapt_own[...])).astype(BF16)
@@ -429,59 +483,111 @@
 
             @pl.when(step == i)
             def _():
-                gather.pump(i - 1, i)
+                gather.pump(i - 1, True)
+                ask(i - 1 + gather.ahead)
+                if i > 1:
+                    gather.relay(i - 2, True)
+                if i > 2:
+                    gather.relay_last(i - 3)
 
         return carry
-
-    lax.fori_loop(0, 4, attend_pack, 0)
-    w.ctx_in[0] = w.ctx_out[0]
-    h_copy.wait()
-    for k in (1, 2, 3):
-        context_to(k).wait_recv()
-    gather.to_core(1).wait_recv()
-    gather.landed(0, 1)
-    attention_out(w.h_v, w.ctx_in, gains, biases, w, False)
-    gather.adapt_far().wait_recv()
-    gather.adapt_core().start()
-    ups, downs = 1 + gather.cuts, 1 + 2 * gather.cuts
-    gather.pump(3, ups - 1)
-    for i in (2, 3):
-        gather.to_core(i).wait_recv()
-
-    def rest_of_up(slot):
-        @pl.when(slot == 2)
-        def _():
-            gather.pump(ups - 1, ups + 1)
-            gather.landed(1, ups)
-
-    feedforward_up(w, False, rest_of_up)
-    gather.pump(ups + 1, ups + 2)
-    for part in blocks_of(rows, 256):
-        w.acc[part] += nn(w.act_v[0, part], w.ff_v[1, 0]) + nn(w.act_v[1, part], w.ff_v[1, 1])
-    gather.pump(ups + 2, downs + 1)
-    gather.landed(ups, downs)
 
     def hop(way, i, src, dst):
         return remote(src, dst, w.hop_send.at[way, i], w.hop_recv.at[way, i], beyond)
 
-    pieces = blocks_of(rows, 128)
-    for i, part in enumerate(pieces):
-        total = w.acc[part] + nn(w.act_v[2, part], w.ff_v[1, 2]) + nn(w.act_v[3, part], w.ff_v[1, 3])
-        w.hop_v[part] = (normalize(total)[0] * gains[1:2] + biases[1:2]).astype(BF16)
-        hop(0, i, w.hop_v.at[part], w.recv_v.at[part]).start()
-    gather.pump(downs + 1, gather.count)
-    gather.relay(gather.count - 1)
+    def ask(i):
+        if i < gather.items:
+            gather.issue(i, i < gather.through)
+
+    @pl.when(section == 0)
+    def _():
+        for i in range(gather.ahead):
+            ask(i)
+        lax.fori_loop(0, 4, attend_pack, 0)
+        w.ctx_in[0] = w.ctx_out[0]
+        gather.adapt_far().wait_recv()
+        gather.adapt_core().start()
+        for k in (1, 2, 3):
+            context_to(k).wait_recv()
+        gather.to_core(1).wait_recv()
+        gather.landed(0)
+        attention_out(w.h_v, w.ctx_in, gains, biases, w, False)
+        gather.pump(3, True)
+        ask(3 + gather.ahead)
+        gather.relay(2, True)
+        gather.relay_last(1)
+        for i in (2, 3):
+            gather.to_core(i).wait_recv()
+
+        def rest_of_up(slot):
+            @pl.when(slot == 2)
+            def _():
+                gather.relay_last(2)
+                gather.landed(1, 2)
+
+            @pl.when(slot == 3)
+            def _():
+                gather.pump(4, True)
+                ask(4 + gather.ahead)
+                gather.relay(3, True)
+
+        feedforward_up(w, False, rest_of_up)
+        gather.relay_last(3)
+        for part in blocks_of(rows, 256):
+            w.acc[part] += nn(w.act_v[0, part], w.ff_v[1, 0]) + nn(w.act_v[1, part], w.ff_v[1, 1])
+        gather.relay(4, True)
+        gather.relay_last(4)
+        gather.landed(3, 4)
+        for i, part in enumerate(pieces):
+            total = w.acc[part]
+            for slot in (2, 3):
+                total = total + nn(w.act_v[slot, part], w.ff_v[1, slot])
+            w.hop_v[part] = (normalize(total)[0] * gains[1:2] + biases[1:2]).astype(BF16)
+            hop(0, i, w.hop_v.at[part], w.recv_v.at[part]).start()
+        for i in range(5, gather.items):
+            gather.pump(i, False)
+            ask(i + gather.ahead)
+            if i > 5:
+                gather.relay(i - 1, False)
+        gather.relay(gather.items - 1, False)
+
+    order = (5, 6, 7, 0, 1, 2, 3, 4)
+
+    def own_step(n):
+        gather.pump(order[n], False)
+        if n + gather.ahead_own < gather.items:
+            gather.issue(order[n + gather.ahead_own], False)
+        if n > 0:
+            gather.relay(order[n - 1], False)
+
+    @pl.when(section == 1)
+    def _():
+        mask(tensor)
+        gather.adapt_far().wait_recv()
+        gather.adapt_core().start()
+        for n in range(gather.ahead_own):
+            gather.issue(order[n], False)
+        for i in range(gather.through):
+            gather.help(i)
+            if i > 1:
+                own_step(i - 2)
+        for n in (3, 4, 5):
+            own_step(n)
+        for i in range(gather.through):
+            gather.to_beyond(i).wait_send()
+        gather.to_core(1).wait_recv()
+        gather.landed(0)
+
     for i in (0, 4):
         gather.to_core(i).wait_recv()
     gather.adapt_core().wait_recv()
-    gather.landed(downs, gather.count)
+    gather.landed(5, 6, 7)
 
     def ready(part):
-        for i in range(part.start // 128, (part.start + part.size) // 128):
-            hop(0, i, w.hop_v.at[pieces[i]], w.recv_v.at[pieces[i]]).wait_recv()
-
         @pl.when(section == 1)
         def _():
+            for i in range(part.start // 128, (part.start + part.size) // 128):
+                hop(0, i, w.hop_v.at[pieces[i]], w.recv_v.at[pieces[i]]).wait_recv()
             w.h_v[part] = w.recv_v[part]
 
     project(w.h_v, adapt_down, w, ready)
@@ -495,48 +601,75 @@
                 w.p_v[g * (w.q_v.shape[2] // HEAD_DIM) + head, part] = value
 
         attend(w.q_v.at[g], w.k_v[g], w.v_v[g], w.bias, give)
+        @pl.when(jnp.logical_and(section == 1, g == 0))
+        def _():
+            own_step(6)
+
         return carry
 
     lax.fori_loop(0, groups, attend_group, 0)
     attention_out(w.h_v, w.ctx_v, gains, biases, w, True)
-    feedforward_up(w, True, lambda slot: None)
-
-    def block(out, index, i):
-        return out.at[pl.ds(index * rows + i * 128, 128)]
-
-    def rows_far(n, src, out, i):
-        return remote(
-            src.at[pieces[i]], block(out, tensor, i), w.row_send.at[n, 0, i], w.row_recv.at[n, 0, i], far
-        )
-
-    def rows_core(n, src, out, i):
-        return remote(
-            src.at[pieces[i]], block(out, tensor, i), w.row_send.at[n, 1, i], w.row_recv.at[n, 1, i], core
-        )
-
-    def rows_mine(n, src, out, i):
-        return pltpu.make_async_copy(src.at[pieces[i]], block(out, tensor, i), w.local.at[7 + 4 * n + i])
-
-    def rows_relay(n, out, i):
-        landed = block(out, turned, i)
+
+    @pl.when(section == 1)
+    def _():
+        own_step(7)
+        for i in (2, 3):
+            gather.to_core(i).wait_recv()
+        gather.landed(1, 2)
+
+    def rest_of_down(slot):
+        @pl.when(jnp.logical_and(section == 1, slot == 3))
+        def _():
+            gather.relay(order[7], False)
+
+    feedforward_up(w, True, rest_of_down)
+
+    @pl.when(section == 1)
+    def _():
+        gather.landed(3, 4)
+
+    def block(out, index, part):
+        return out.at[pl.ds(index * rows + part.start, part.size)]
+
+    def rows_to(n, way, i, src, out, part, device):
+        sems = w.row_send.at[n, way, i], w.row_recv.at[n, way, i]
+        return remote(src.at[part], block(out, tensor, part), *sems, device)
+
+    def rows_far(n, i, src, out, part):
+        return rows_to(n, 0, i, src, out, part, far)
+
+    def rows_core(n, i, src, out, part):
+        return rows_to(n, 1, i, src, out, part, core)
+
+    def rows_mine(n, i, src, out, part):
+        return pltpu.make_async_copy(src.at[part], block(out, tensor, part), w.local.at[7 + 4 * n + i])
+
+    def rows_relay(n, i, out, part):
+        landed = block(out, turned, part)
         return remote(landed, landed, w.row_send.at[n, 2, i], w.row_recv.at[n, 2, i], core)
 
-    def spread(n, src, out, i):
+    def spread(n, i, src, out, part):
         for make in (rows_far, rows_core, rows_mine):
-            make(n, src, out, i).start()
-
-    def relay_rows(n, src, out, i):
-        rows_far(n, src, out, i).wait_recv()
-        rows_relay(n, out, i).start()
-
-    def gathered(n, src, out):
-        for i in range(len(pieces)):
-            rows_core(n, src, out, i).wait_recv()
-            rows_relay(n, out, i).wait_recv()
-            for make in (rows_far, rows_core):
-                make(n, src, out, i).wait_send()
-            rows_relay(n, out, i).wait_send()
-            rows_mine(n, src, out, i).wait()
+            make(n, i, src, out, part).start()
+
+    def relay_rows(n, i, src, out, part):
+        rows_far(n, i, src, out, part).wait_recv()
+        rows_relay(n, i, out, part).start()
+
+    def gathered(n, i, src, out, part):
+        rows_core(n, i, src, out, part).wait()
+        rows_relay(n, i, out, part).wait()
+        rows_mine(n, i, src, out, part).wait()
+
+    ends = (pl.ds(0, 128), pl.ds(128, 128), pl.ds(256, rows - 256))
+
+    def through_corner(src):
+        sems = w.row_send.at[1, 1, 3], w.row_recv.at[1, 1, 3]
+        return remote(src.at[ends[0]], w.back_v.at[ends[0]], *sems, corner)
+
+    def through_beyond():
+        sems = w.row_send.at[1, 0, 3], w.row_recv.at[1, 0, 3]
+        return remote(w.back_v.at[ends[0]], block(in_grads, turned, ends[0]), *sems, beyond)
 
     for i, part in enumerate(pieces):
         total = w.acc[part]
@@ -546,19 +679,16 @@
         w.n2_v[part] = normed
         w.s2_v[part] = scaled
         w.layer_v[part] = (normed * gains[1:2] + biases[1:2]).astype(BF16)
-        spread(0, w.layer_v, layer_outs, i)
+        spread(0, i, w.layer_v, layer_outs, part)
 
     cot_copy.wait()
     rank = adapt_down.shape[0] // 2
 
     def incoming(again, part):
-        @pl.when(again == 1)
+        @pl.when(jnp.logical_and(again == 1, section == 0))
         def _():
             for i in range(part.start // 128, (part.start + part.size) // 128):
                 hop(1, i, w.dh_v.at[pieces[i]], w.back_v.at[pieces[i]]).wait_recv()
-
-        @pl.when(jnp.logical_and(again == 1, section == 0))
-        def _():
             w.cot_v[part] = w.back_v[part]
 
         return w.cot_v[part].astype(F32)
@@ -599,15 +729,25 @@
     def hand_over(again, part, value):
         i = part.start // 128
 
-        @pl.when(again == 0)
+        @pl.when(jnp.logical_and(again == 0, section == 1))
         def _():
             w.dh_v[part] = value
             hop(1, i, w.dh_v.at[part], w.back_v.at[part]).start()
-
-        @pl.when(again == 1)
+            for n, end in enumerate(ends):
+                if end.start + end.size == part.start + part.size:
+                    spread(1, n, w.dh_v, in_grads, end)
+
+        @pl.when(jnp.logical_and(again == 1, section == 0))
         def _():
-            w.din_v[part] = value
-            spread(1, w.din_v, in_grads, i)
+            w.dh_v[part] = value
+            for n, end in enumerate(ends):
+                if end.start + end.size == part.start + part.size:
+                    if n:
+                        rows_far(1, n, w.dh_v, in_grads, end).start()
+                    else:
+                        through_corner(w.dh_v).start()
+                    rows_core(1, n, w.dh_v, in_grads, end).start()
+                    rows_mine(1, n, w.dh_v, in_grads, end).start()
 
     def back(again, carry):
         backward(
@@ -621,12 +761,19 @@
 
         @pl.when(again == 0)
         def _():
-            for i in range(len(pieces)):
-                relay_rows(0, w.layer_v, layer_outs, i)
+            for i, part in enumerate(pieces):
+                relay_rows(0, i, w.layer_v, layer_outs, part)
 
         return carry
 
     lax.fori_loop(0, 2, back, 0)
+
+    @pl.when(section == 1)
+    def _():
+        for n, end in enumerate(ends):
+            relay_rows(1, n, w.dh_v, in_grads, end)
+        through_corner(w.dh_v).wait_recv()
+        through_beyond().start()
 
     tensor_copies = over_tensor(True)
     for copy in tensor_copies:
@@ -638,7 +785,11 @@
     for m, device in enumerate(ring):
         for k, ref in enumerate(totals):
             summed(base + 2 * m + k, ref.at[plane], ref.at[plane], device).start()
-    relay_rows(1, w.din_v, in_grads, 0)
+
+    @pl.when(section == 0)
+    def _():
+        relay_rows(1, 1, w.dh_v, in_grads, ends[1])
+
     for m, device in enumerate(ring):
         source = lax.rem(plane + planes - m - 1, planes)
         for k, ref in enumerate(totals):
@@ -652,16 +803,35 @@
         up_total = up_total + w.plane_up[m]
     up_out[...] = up_total
     down_out[...] = down_total
-    for i in range(1, len(pieces)):
-        relay_rows(1, w.din_v, in_grads, i)
-    for way, src, dst in ((0, w.hop_v, w.recv_v), (1, w.dh_v, w.back_v)):
+
+    @pl.when(section == 0)
+    def _():
+        through_beyond().wait_recv()
+        rows_relay(1, 0, in_grads, ends[0]).start()
+        relay_rows(1, 2, w.dh_v, in_grads, ends[2])
+        through_corner(w.dh_v).wait_send()
+        for n in (1, 2):
+            rows_far(1, n, w.dh_v, in_grads, ends[n]).wait_send()
         for i, part in enumerate(pieces):
-            hop(way, i, src.at[part], dst.at[part]).wait_send()
-    gather.sent()
-    for k in (1, 2, 3):
-        context_to(k).wait_send()
-    gathered(0, w.layer_v, layer_outs)
-    gathered(1, w.din_v, in_grads)
+            hop(0, i, w.hop_v.at[part], w.recv_v.at[part]).wait_send()
+        for k in (1, 2, 3):
+            context_to(k).wait_send()
+        gather.sent(0)
+
+    @pl.when(section == 1)
+    def _():
+        through_beyond().wait_send()
+        for n, end in enumerate(ends):
+            rows_far(1, n, w.dh_v, in_grads, end).wait_send()
+        for i, part in enumerate(pieces):
+            hop(1, i, w.dh_v.at[part], w.back_v.at[part]).wait_send()
+        gather.sent(1)
+
+    for i, part in enumerate(pieces):
+        rows_far(0, i, w.layer_v, layer_outs, part).wait_send()
+        gathered(0, i, w.layer_v, layer_outs, part)
+    for n, end in enumerate(ends):
+        gathered(1, n, w.dh_v, in_grads, end)
 
 
 def local(
@@ -722,8 +892,8 @@
         plane_up=pltpu.VMEM((planes, *up_part), F32),
         local=pltpu.SemaphoreType.DMA((15,)),
         packs=pltpu.SemaphoreType.DMA((packs,)),
-        send=pltpu.SemaphoreType.DMA((6, Gather.count)),
-        recv=pltpu.SemaphoreType.DMA((6, Gather.count)),
+        send=pltpu.SemaphoreType.DMA((11, Gather.items)),
+        recv=pltpu.SemaphoreType.DMA((11, Gather.items)),
         ctx_send=pltpu.SemaphoreType.DMA((slots,)),
         ctx_recv=pltpu.SemaphoreType.DMA((slots,)),
         hop_send=pltpu.SemaphoreType.DMA((2, rows // 128)),
@@ -734,7 +904,7 @@
         sum_recv=pltpu.SemaphoreType.DMA((sums,)),
     )
     scratch |= dict.fromkeys(("h_v", "recv_v", "back_v", "cot_v", "low_v"), low_rows)
-    scratch |= dict.fromkeys(("hop_v", "layer_v", "dh_v", "din_v"), low_rows)
+    scratch |= dict.fromkeys(("hop_v", "layer_v", "dh_v"), low_rows)
     scratch |= dict.fromkeys(("acc", "n1_v", "n2_v"), full_rows)
     scratch |= dict.fromkeys(("q_v", "k_v", "v_v", "ctx_v"), of_heads)
     scratch |= dict.fromkeys(("dq_v", "dk_v", "dv_v", "dctx_v"), of_heads)

time: 175 us -> 172 us (0.983)
  Pallas kernels: 169 us -> 166 us
    pallas_call x1, Pallas kernels: 169 us -> 166 us  [local(): pl.pallas_call(partial(whole_kernel, planes, tuple(scratch)), name='encod...]
where the time goes in v1:
time: 172 us; the launch traced here: 171 us
  Pallas kernels  166 us (97%)
  local copies, waits for them, and re-layouts  4.56 us (3%)
    pallas_call x1, Pallas kernels, local(): pl.pallas_call(partial(whole_kernel, planes, tuple(scratch)), name='encod...  166 us
    unnamed x8, local copies, waits for them, and re-layouts  4.56 us

profile of v1, /device:TPU:0, one launch (start us, length us, event | category | flops | bytes accessed | tf_op | source)
XLA Modules:
  0.0 171.0 jit_solution(16898956971112913958)
XLA Ops:
  0.6 165.8 %encoder_layers.1 = (bf16[2048,768]{1,0:T(8,128)(2,1)S(1)}, bf16[2048,768]{1,0:T(8,128)(2,1)S(1)}, f32[2,8,768]{2,1,0:T(8,128)}, f32[2,8,192]{2,1,0:T(8,128)}) custom-call(bf16[2048,768]{1,0:T(8,128)(2,1)} %refs_0_.1, s32[4,512]{1,0:T(4,128)} %refs_1_.1, f32[2,768]{1,0:T(2,128)} %bitcast.30, f32[2,768]{1,0:T(2,128)} %bitcast.31, bf16[16,768]{1,0:T(8,128)(2,1)} %bitcast.28, ...), custom_call_target="tpu_custom_call" | custom-call | flops 70000001024 | bytes 30000000 | tf_op jit(solution)/shard_map/encoder_layers/pallas_call | solution.py:912
  166.4 1.7 copy.19
  168.1 0.0 copy-start
  168.1 0.0 copy-start.1
  168.1 1.7 copy.20
  169.8 0.0 copy-done
  169.8 0.6 copy.21
  170.4 0.0 copy-done.1
  170.4 0.6 copy.22
Async XLA Ops:
  168.1 1.7 copy-start
  168.1 2.3 %copy-start.1 = (f32[2,8,192]{2,1,0:T(8,128)S(1)}, f32[2,8,192]{2,1,0:T(8,128)}, u32[]{:S(2)}) copy-start(f32[2,8,192]{2,1,0:T(8,128)} %get-tuple-element.11) | copy-start | bytes 36868

commit v2 on v1

--- a/solution.py
+++ b/solution.py
@@ -377,7 +377,7 @@
         dmid = 2.0 * jnp.where(lane_mask(dmid_q.shape, 0, rank), dmid_q, dmid_v)
         w.dmid_v[part] = dmid.astype(BF16)
     sums()
-    for part in blocks_of(rows, 128):
+    for part in blocks_of(rows, 256):
         total = w.acc[part]
         for g in range(groups):
             cols = slice(g * span, (g + 1) * span)
@@ -441,7 +441,7 @@
     h_copy.wait()
     square = (rows, rows)
     piece = adapt.shape[1]
-    pieces = blocks_of(rows, 128)
+    pieces = blocks_of(rows, 256)
 
     def mask(pack):
         diagonal = lax.broadcasted_iota(jnp.int32, square, 0) == lax.broadcasted_iota(
@@ -569,9 +569,9 @@
             gather.issue(order[n], False)
         for i in range(gather.through):
             gather.help(i)
-            if i > 1:
-                own_step(i - 2)
-        for n in (3, 4, 5):
+            if i > 0:
+                own_step(i - 1)
+        for n in (4, 5, 6):
             own_step(n)
         for i in range(gather.through):
             gather.to_beyond(i).wait_send()
@@ -586,8 +586,7 @@
     def ready(part):
         @pl.when(section == 1)
         def _():
-            for i in range(part.start // 128, (part.start + part.size) // 128):
-                hop(0, i, w.hop_v.at[pieces[i]], w.recv_v.at[pieces[i]]).wait_recv()
+            hop(0, part.start // 256, w.hop_v.at[part], w.recv_v.at[part]).wait_recv()
             w.h_v[part] = w.recv_v[part]
 
     project(w.h_v, adapt_down, w, ready)
@@ -603,7 +602,8 @@
         attend(w.q_v.at[g], w.k_v[g], w.v_v[g], w.bias, give)
         @pl.when(jnp.logical_and(section == 1, g == 0))
         def _():
-            own_step(6)
+            own_step(7)
+
 
         return carry
 
@@ -612,7 +612,6 @@
 
     @pl.when(section == 1)
     def _():
-        own_step(7)
         for i in (2, 3):
             gather.to_core(i).wait_recv()
         gather.landed(1, 2)
@@ -687,8 +686,7 @@
     def incoming(again, part):
         @pl.when(jnp.logical_and(again == 1, section == 0))
         def _():
-            for i in range(part.start // 128, (part.start + part.size) // 128):
-                hop(1, i, w.dh_v.at[pieces[i]], w.back_v.at[pieces[i]]).wait_recv()
+            hop(1, part.start // 256, w.dh_v.at[part], w.back_v.at[part]).wait_recv()
             w.cot_v[part] = w.back_v[part]
 
         return w.cot_v[part].astype(F32)
@@ -727,27 +725,25 @@
                 copy.start()
 
     def hand_over(again, part, value):
-        i = part.start // 128
+        here = [n for n, end in enumerate(ends) if 0 <= end.start - part.start < part.size]
 
         @pl.when(jnp.logical_and(again == 0, section == 1))
         def _():
             w.dh_v[part] = value
-            hop(1, i, w.dh_v.at[part], w.back_v.at[part]).start()
-            for n, end in enumerate(ends):
-                if end.start + end.size == part.start + part.size:
-                    spread(1, n, w.dh_v, in_grads, end)
+            hop(1, part.start // 256, w.dh_v.at[part], w.back_v.at[part]).start()
+            for n in here:
+                spread(1, n, w.dh_v, in_grads, ends[n])
 
         @pl.when(jnp.logical_and(again == 1, section == 0))
         def _():
             w.dh_v[part] = value
-            for n, end in enumerate(ends):
-                if end.start + end.size == part.start + part.size:
-                    if n:
-                        rows_far(1, n, w.dh_v, in_grads, end).start()
-                    else:
-                        through_corner(w.dh_v).start()
-                    rows_core(1, n, w.dh_v, in_grads, end).start()
-                    rows_mine(1, n, w.dh_v, in_grads, end).start()
+            for n in here:
+                if n:
+                    rows_far(1, n, w.dh_v, in_grads, ends[n]).start()
+                else:
+                    through_corner(w.dh_v).start()
+                rows_core(1, n, w.dh_v, in_grads, ends[n]).start()
+                rows_mine(1, n, w.dh_v, in_grads, ends[n]).start()
 
     def back(again, carry):
         backward(

time: 172 us -> 166 us (0.965)
  Pallas kernels: 166 us -> 161 us
    pallas_call x1, Pallas kernels: 166 us -> 161 us  [local(): pl.pallas_call(partial(whole_kernel, planes, tuple(scratch)), name='encod...]
where the time goes in v2:
time: 166 us
  Pallas kernels  161 us (97%)
  local copies, waits for them, and re-layouts  4.56 us (3%)
    pallas_call x1, Pallas kernels, local(): pl.pallas_call(partial(whole_kernel, planes, tuple(scratch)), name='encod...  161 us
    unnamed x8, local copies, waits for them, and re-layouts  4.56 us

profile of v2, /device:TPU:0, one launch (start us, length us, event | category | flops | bytes accessed | tf_op | source)
XLA Modules:
  0.0 165.9 jit_solution(12796596812914212542)
XLA Ops:
  0.6 160.6 %encoder_layers.1 = (bf16[2048,768]{1,0:T(8,128)(2,1)S(1)}, bf16[2048,768]{1,0:T(8,128)(2,1)S(1)}, f32[2,8,768]{2,1,0:T(8,128)}, f32[2,8,192]{2,1,0:T(8,128)}) custom-call(bf16[2048,768]{1,0:T(8,128)(2,1)} %refs_0_.1, s32[4,512]{1,0:T(4,128)} %refs_1_.1, f32[2,768]{1,0:T(2,128)} %bitcast.30, f32[2,768]{1,0:T(2,128)} %bitcast.31, bf16[16,768]{1,0:T(8,128)(2,1)} %bitcast.28, ...), custom_call_target="tpu_custom_call" | custom-call | flops 70000001024 | bytes 30000000 | tf_op jit(solution)/shard_map/encoder_layers/pallas_call | solution.py:908
  161.3 1.7 %copy.19 = bf16[1,2048,768]{2,1,0:T(8,128)(2,1)} copy(bf16[1,2048,768]{2,1,0:T(8,128)(2,1)S(1)} %bitcast.21) | data formatting | bytes 6291456
  163.0 0.0 copy-start
  163.0 0.0 copy-start.1
  163.0 1.7 %copy.20 = bf16[1,2048,768]{2,1,0:T(8,128)(2,1)} copy(bf16[1,2048,768]{2,1,0:T(8,128)(2,1)S(1)} %bitcast.20) | data formatting | bytes 6291456
  164.6 0.0 copy-done
  164.6 0.6 copy.21
  165.2 0.0 copy-done.1
  165.3 0.6 copy.22
Async XLA Ops:
  163.0 1.7 %copy-start = (f32[2,8,768]{2,1,0:T(8,128)S(1)}, f32[2,8,768]{2,1,0:T(8,128)}, u32[]{:S(2)}) copy-start(f32[2,8,768]{2,1,0:T(8,128)} %get-tuple-element.10) | copy-start | bytes 147460
  163.0 2.3 %copy-start.1 = (f32[2,8,192]{2,1,0:T(8,128)S(1)}, f32[2,8,192]{2,1,0:T(8,128)}, u32[]{:S(2)}) copy-start(f32[2,8,192]{2,1,0:T(8,128)} %get-tuple-element.11) | copy-start | bytes 36868

commit v3 on v2

--- a/solution.py
+++ b/solution.py
@@ -303,18 +303,32 @@
 
 
 def feedforward_up(w, keep, ready):
-    def step(slot, carry):
+    rows = w.low_v.shape[0]
+
+    def one(slot, part):
+        pre = nn(w.low_v[part], w.ff_v[0, slot])
+        cdf = 0.5 + 0.5 * lax.erf(pre * (0.5**0.5))
+        w.act_v[slot, part] = (pre * cdf).astype(BF16)
+        if keep:
+            density = jnp.exp(pre * pre * -0.5) * 0.3989422804014327
+            w.slope_v[slot, part] = (cdf + pre * density).astype(BF16)
+
+    def small_step(slot, carry):
         ready(slot)
-        for part in blocks_of(w.low_v.shape[0], 128):
-            pre = nn(w.low_v[part], w.ff_v[0, slot])
-            cdf = 0.5 + 0.5 * lax.erf(pre * (0.5**0.5))
-            w.act_v[slot, part] = (pre * cdf).astype(BF16)
-            if keep:
-                density = jnp.exp(pre * pre * -0.5) * 0.3989422804014327
-                w.slope_v[slot, part] = (cdf + pre * density).astype(BF16)
-        return carry
-
-    lax.fori_loop(0, w.act_v.shape[0], step, 0)
+
+        def some(i, carry):
+            one(slot, pl.ds(pl.multiple_of(i * 256, 256), 256))
+            return carry
+
+        return lax.fori_loop(0, rows // 256, some, carry)
+
+    if keep:
+        for slot in range(w.act_v.shape[0]):
+            ready(jnp.int32(slot))
+            for part in blocks_of(rows, 128):
+                one(slot, part)
+    else:
+        lax.fori_loop(0, w.act_v.shape[0], small_step, 0)
 
 
 def backward(w, gains, adapt_down, incoming, give, sums):
@@ -331,7 +345,8 @@
             w.act_v[slot, part] = (dact * w.slope_v[slot, part].astype(F32)).astype(BF16)
             return carry
 
-        lax.fori_loop(0, slots, step, 0)
+        for slot in range(slots):
+            step(slot, 0)
         total = w.acc[part]
         for slot in range(slots):
             total = total + nt(w.act_v[slot, part], w.ff_v[0, slot])

time: 166 us -> 163 us (0.982)
  Pallas kernels: 161 us -> 157 us
    pallas_call x1, Pallas kernels: 161 us -> 157 us  [local(): pl.pallas_call(partial(whole_kernel, planes, tuple(scratch)), name='encod...]
where the time goes in v3:
time: 163 us; the launch traced here: 162 us
  Pallas kernels  157 us (96%)
  local copies, waits for them, and re-layouts  4.56 us (3%)
    pallas_call x1, Pallas kernels, local(): pl.pallas_call(partial(whole_kernel, planes, tuple(scratch)), name='encod...  157 us
    unnamed x8, local copies, waits for them, and re-layouts  4.56 us

profile of v3, /device:TPU:0, one launch (start us, length us, event | category | flops | bytes accessed | tf_op | source)
XLA Modules:
  0.0 162.2 jit_solution(14535133069093381880)
XLA Ops:
  0.6 157.0 %encoder_layers.1 = (bf16[2048,768]{1,0:T(8,128)(2,1)S(1)}, bf16[2048,768]{1,0:T(8,128)(2,1)S(1)}, f32[2,8,768]{2,1,0:T(8,128)}, f32[2,8,192]{2,1,0:T(8,128)}) custom-call(bf16[2048,768]{1,0:T(8,128)(2,1)} %refs_0_.1, s32[4,512]{1,0:T(4,128)} %refs_1_.1, f32[2,768]{1,0:T(2,128)} %bitcast.30, f32[2,768]{1,0:T(2,128)} %bitcast.31, bf16[16,768]{1,0:T(8,128)(2,1)} %bitcast.28, ...), custom_call_target="tpu_custom_call" | custom-call | flops 70000001024 | bytes 30000000 | tf_op jit(solution)/shard_map/encoder_layers/pallas_call | solution.py:923
  157.7 1.7 %copy.19 = bf16[1,2048,768]{2,1,0:T(8,128)(2,1)} copy(bf16[1,2048,768]{2,1,0:T(8,128)(2,1)S(1)} %bitcast.21) | data formatting | bytes 6291456
  159.3 0.0 copy-start
  159.3 0.0 copy-start.1
  159.3 1.7 %copy.20 = bf16[1,2048,768]{2,1,0:T(8,128)(2,1)} copy(bf16[1,2048,768]{2,1,0:T(8,128)(2,1)S(1)} %bitcast.20) | data formatting | bytes 6291456
  161.0 0.0 copy-done
  161.0 0.6 copy.21
  161.6 0.0 copy-done.1
  161.6 0.6 copy.22
Async XLA Ops:
  159.3 1.7 %copy-start = (f32[2,8,768]{2,1,0:T(8,128)S(1)}, f32[2,8,768]{2,1,0:T(8,128)}, u32[]{:S(2)}) copy-start(f32[2,8,768]{2,1,0:T(8,128)} %get-tuple-element.10) | copy-start | bytes 147460
  159.3 2.3 %copy-start.1 = (f32[2,8,192]{2,1,0:T(8,128)S(1)}, f32[2,8,192]{2,1,0:T(8,128)}, u32[]{:S(2)}) copy-start(f32[2,8,192]{2,1,0:T(8,128)} %get-tuple-element.11) | copy-start | bytes 36868

commit v4 on v3

--- a/solution.py
+++ b/solution.py
@@ -264,11 +264,11 @@
                 ref[g, part] = value[:, g * span : (g + 1) * span]
 
 
-def attend(q_v, k, v, bias, give):
+def attend(q_v, k, v, bias, give, small=False):
     rows, span = k.shape
     chunk = 256
     zero = jnp.zeros((), BF16)
-    for part in blocks_of(rows, chunk):
+    def some(part):
         q_c = q_v[part] * jnp.asarray(HEAD_DIM**-0.5, BF16)
         ctx = jnp.zeros((chunk, span), F32)
         inverse = jnp.zeros((chunk, span), F32)
@@ -285,6 +285,17 @@
             inverse = jnp.where(of_head, scale, inverse)
             give(part, e, weight, None)
         give(part, None, ctx.astype(BF16), inverse)
+
+    if small:
+
+        def step(i, carry):
+            some(pl.ds(pl.multiple_of(i * chunk, chunk), chunk))
+            return carry
+
+        lax.fori_loop(0, rows // chunk, step, 0)
+    else:
+        for part in blocks_of(rows, chunk):
+            some(part)
 
 
 def attention_out(h_v, context, gains, biases, w, keep):
@@ -381,7 +392,8 @@
         w.dv_v[g] = jnp.concatenate(dv_t, 0).astype(BF16).T
         return carry
 
-    lax.fori_loop(0, groups, group, 0)
+    for g in range(groups):
+        group(g, 0)
     rank = adapt_down.shape[0] // 2
     for part in blocks_of(rows, 256):
         dmid_q = dmid_v = 0.0
@@ -488,7 +500,7 @@
             if head is None:
                 w.ctx_out[k, part] = value
 
-        attend(w.q_own, k_own, v_own, w.bias, give)
+        attend(w.q_own, k_own, v_own, w.bias, give, True)
 
         @pl.when(step < 3)
         def _():

time: 163 us -> 162 us (level)
  no operation moved by 1% of the time
where the time goes in v4:
time: 162 us; the launch traced here: 161 us
  Pallas kernels  156 us (96%)
  local copies, waits for them, and re-layouts  4.56 us (3%)
    pallas_call x1, Pallas kernels, local(): pl.pallas_call(partial(whole_kernel, planes, tuple(scratch)), name='encod...  156 us
    unnamed x8, local copies, waits for them, and re-layouts  4.56 us

profile of v4, /device:TPU:0, one launch (start us, length us, event | category | flops | bytes accessed | tf_op | source)
XLA Modules:
  0.0 160.8 jit_solution(10520697452565244443)
XLA Ops:
  0.6 155.6 %encoder_layers.1 = (bf16[2048,768]{1,0:T(8,128)(2,1)S(1)}, bf16[2048,768]{1,0:T(8,128)(2,1)S(1)}, f32[2,8,768]{2,1,0:T(8,128)}, f32[2,8,192]{2,1,0:T(8,128)}) custom-call(bf16[2048,768]{1,0:T(8,128)(2,1)} %refs_0_.1, s32[4,512]{1,0:T(4,128)} %refs_1_.1, f32[2,768]{1,0:T(2,128)} %bitcast.30, f32[2,768]{1,0:T(2,128)} %bitcast.31, bf16[16,768]{1,0:T(8,128)(2,1)} %bitcast.28, ...), custom_call_target="tpu_custom_call" | custom-call | flops 70000001024 | bytes 30000000 | tf_op jit(solution)/shard_map/encoder_layers/pallas_call | solution.py:935
  156.2 1.7 %copy.19 = bf16[1,2048,768]{2,1,0:T(8,128)(2,1)} copy(bf16[1,2048,768]{2,1,0:T(8,128)(2,1)S(1)} %bitcast.21) | data formatting | bytes 6291456
  157.9 0.0 copy-start
  157.9 0.0 copy-start.1
  157.9 1.7 %copy.20 = bf16[1,2048,768]{2,1,0:T(8,128)(2,1)} copy(bf16[1,2048,768]{2,1,0:T(8,128)(2,1)S(1)} %bitcast.20) | data formatting | bytes 6291456
  159.6 0.0 copy-done
  159.6 0.6 copy.21
  160.2 0.0 copy-done.1
  160.2 0.6 copy.22
Async XLA Ops:
  157.9 1.7 %copy-start = (f32[2,8,768]{2,1,0:T(8,128)S(1)}, f32[2,8,768]{2,1,0:T(8,128)}, u32[]{:S(2)}) copy-start(f32[2,8,768]{2,1,0:T(8,128)} %get-tuple-element.10) | copy-start | bytes 147460
  157.9 2.3 %copy-start.1 = (f32[2,8,192]{2,1,0:T(8,128)S(1)}, f32[2,8,192]{2,1,0:T(8,128)}, u32[]{:S(2)}) copy-start(f32[2,8,192]{2,1,0:T(8,128)} %get-tuple-element.11) | copy-start | bytes 36868
